TPU v7x, 32 devices: a whole 2x2x4 slice. The times are simulated.
32 devices in a mesh: seq: 16 (over z, y, x), tp: 2 (over core).
Axes of the slice: x: 2, y: 2, z: 4, core: 2. Of those that a mesh axis runs over, the one named last changes fastest.
Arguments:
- segment_ids: int32 [4096], replicated, may hold values from 0 to 7, never falling along the last dimension, each value on 1 to 1024 neighbouring positions
- relayout: int32 [4096], replicated, may hold values from 0 to 4095, as said below
- queries: bfloat16 [4096, 4096], P('seq', 'tp'), may hold values from -8 to 8
- keys: bfloat16 [4096, 512], P(('seq', 'tp')), may hold values from -8 to 8
- values: bfloat16 [4096, 512], P(('seq', 'tp')), may hold values from -18 to 18
- out_weight: bfloat16 [4096, 8192], P('tp'), may hold values from -0.09375 to 0.09375
Outputs:
- block_out: bfloat16 [4096, 8192], P(('seq', 'tp'))
Inputs may be any that keep to these rules, and one draw needn't show every extreme that they name: relayout is a permutation; of the 256 tokens in each aligned block of 256 initial positions exactly 16 land in each aligned block of 256 new positions.
All inputs are finite; a program needn't handle non-finite values.
Results may differ from a plain program's by a relative error of at most 0.017.
Values may be sent and summed in bfloat16 or wider, within the bound.
A program may use at most 192 MiB of HBM per device.

v0:
```python
import jax
import jax.numpy as jnp
from jax import lax
from jax.sharding import PartitionSpec as P

QH = 32
KVH = 4
HD = 128


def shards(segment_ids, relayout, queries, keys, values, out_weight):
    rows_here = queries.shape[0]
    seq_count = lax.axis_size("seq")
    seq_index = lax.axis_index("seq")
    tp_index = lax.axis_index("tp")
    total_rows = rows_here * seq_count
    heads_here = queries.shape[1] // HD
    group = QH // KVH
    shared_here = max(1, heads_here // group)
    per_shared = heads_here // shared_here
    scale = HD ** (-0.5)
    all_keys, all_values = (
        lax.all_gather(keys, "tp", axis=0, tiled=True),
        lax.all_gather(values, "tp", axis=0, tiled=True),
    )
    first_head = tp_index * heads_here // group
    own_keys = lax.dynamic_slice_in_dim(all_keys, first_head * HD, shared_here * HD, 1)
    own_values = lax.dynamic_slice_in_dim(all_values, first_head * HD, shared_here * HD, 1)
    own_pair = jnp.stack([own_keys, own_values])
    row_ids = jnp.arange(rows_here, dtype=jnp.int32)
    inverse = (
        jnp.zeros((total_rows,), jnp.int32)
        .at[relayout]
        .set(jnp.arange(total_rows, dtype=jnp.int32))
    )
    new_here = seq_index * rows_here + row_ids
    old_here = seq_index * rows_here + row_ids
    source_block = relayout[new_here] // rows_here
    arrival = jnp.argsort(source_block * total_rows + new_here)
    send_order = jnp.argsort(inverse[old_here])
    arrived = lax.all_to_all(queries[send_order], "seq", split_axis=0, concat_axis=0, tiled=True)
    query_pos = relayout[seq_index * rows_here + arrival]
    query_seg = segment_ids[query_pos]
    pieces = lax.all_gather(own_pair, "seq", axis=1, tiled=True)
    count = pieces.shape[1]
    key_pos = jnp.arange(count, dtype=jnp.int32)
    live = (
        (key_pos[None, :] <= query_pos[:, None])
        & (segment_ids[None, :] == query_seg[:, None])
        & (jnp.int32(0) >= 0)
    )
    query_split = arrived.reshape(rows_here, shared_here, per_shared, HD)
    key_split = pieces[0].reshape(count, shared_here, HD)
    value_split = pieces[1].reshape(count, shared_here, HD)
    scores = (
        jnp.einsum("qngd,knd->ngqk", query_split, key_split, preferred_element_type=jnp.float32)
        * scale
    )
    masked = jnp.where(live, scores, jnp.float32(-1e30))
    peak = jnp.full((shared_here, per_shared, rows_here), -1e30, jnp.float32)
    new_peak = jnp.maximum(peak, jnp.max(masked, axis=-1))
    expo = jnp.where(live, jnp.exp(masked - new_peak[..., None]), jnp.float32(0.0))
    denom = jnp.sum(expo, axis=-1)
    update = jnp.einsum(
        "ngqk,knd->ngqd", expo.astype(jnp.bfloat16), value_split, preferred_element_type=jnp.float32
    )
    attn = update / denom[..., None]
    attn_rows = (
        jnp.transpose(attn, (2, 0, 1, 3)).reshape(rows_here, heads_here * HD).astype(jnp.bfloat16)
    )
    attn_new = jnp.zeros_like(attn_rows).at[arrival].set(attn_rows)
    return lax.psum_scatter(
        jnp.dot(attn_new, out_weight, preferred_element_type=jnp.float32).astype(jnp.bfloat16),
        "tp",
        scatter_dimension=0,
        tiled=True,
    )


def solution(mesh):
    return jax.shard_map(
        shards,
        mesh=mesh,
        in_specs=(
            P(),
            P(),
            P("seq", "tp"),
            P(("seq", "tp"), None),
            P(("seq", "tp"), None),
            P("tp", None),
        ),
        out_specs=P(("seq", "tp"), None),
        check_vma=False,
    )
```

profile of v0, /device:TPU:15, one launch (start us, length us, event | category | flops | bytes accessed | tf_op | source)
XLA Modules:
  0.0 226.2 jit_solution(9249162262679532605)
XLA Ops:
  6.5 0.0 copy-start
  6.5 0.0 all-gather.2.cloned.1.call-start
  6.5 2.6 %all_gather.9 = bf16[256,512]{1,0:T(8,128)(2,1)S(1)} all-gather(bf16[128,512]{1,0:T(8,128)(2,1)} %param.9), channel_id=1, replica_groups=mesh['seq'=16,'tp'=2] {'tp'}, dimensions={0}, use_global_device_ids=true | all-gather | bytes 393216 | tf_op jit(solution)/shard_map/all_gather | solution.py:23
  9.2 2.2 all_gather.10
  11.4 0.7 pad_maximum_fusion
  12.1 0.0 all-gather.2.cloned.1.call-update
  12.2 0.7 compare_select_fusion
  12.9 15.5 %scatter_custom_fusion = s32[4096]{0:T(1024)S(1)} fusion(s32[4096]{0:T(1024)S(1)} %compare_select_fusion, s32[4096]{0:T(1024)S(1)} %iota.23, s32[]{:T(128)} %constant.25.clone.1), kind=kCustom, calls=%fused_computation.28 | custom fusion | bytes 16388 | tf_op jit(solution)/shard_map/scatter | solution.py:34
  28.4 1.7 gather_fusion.3
  30.2 3.2 %sort.32 = (s32[256]{0:T(256)}, s32[256]{0:T(256)S(1)}) sort(s32[256]{0:T(256)S(1)} %gather_fusion.3, s32[256]{0:T(256)S(1)} %iota.24), dimensions={0}, to_apply=%region_2.3 | sort | flops 2048 | bytes 4096 | tf_op jit(solution)/shard_map/jit(argsort)/sort | solution.py:40
  33.4 0.0 copy-done
  33.4 2.3 %gather_fusion.4 = bf16[256,2048]{1,0:T(8,128)(2,1)} fusion(bf16[256,2048]{1,0:T(8,128)(2,1)S(1)} %copy-done, s32[1024]{0:T(1024)S(1)} %pad_clamp_fusion), kind=kCustom, calls=%fused_computation.4 | custom fusion | bytes 2098176 | tf_op jit(solution)/shard_map/gather | solution.py:41
  35.7 6.6 %all-to-all-start = ((bf16[16,16,2048]{2,1,0:T(8,128)(2,1)}), bf16[16,16,2048]{2,1,0:T(8,128)(2,1)S(1)}, u32[]{:S(2)}, u32[]{:S(2)}) async-start(bf16[16,16,2048]{2,1,0:T(8,128)(2,1)} %bitcast.7), calls=%async_computation | async-start | bytes 2097152 | tf_op jit(solution)/shard_map/all_to_all | solution.py:41
  42.3 0.0 reduce-scatter.2.cloned.1.call-start
  42.3 2.0 gather_fusion
  44.3 3.2 %sort.31 = (s32[256]{0:T(256)}, s32[256]{0:T(256)S(1)}) sort(s32[256]{0:T(256)S(1)} %add_add_fusion, s32[256]{0:T(256)S(1)} %iota.22), dimensions={0}, to_apply=%region_0.1 | sort | flops 2048 | bytes 4096 | tf_op jit(solution)/shard_map/jit(argsort)/sort | solution.py:39
  47.5 2.0 gather_fusion.1
  49.5 2.0 gather_fusion.2
  51.4 3.4 %fusion.6 = pred[256,4096]{0,1:T(8,128)(4,1)} fusion(s32[256]{0:T(256)S(1)} %gather_fusion.2, s32[256]{0:T(256)S(1)} %gather_fusion.1, s32[4096]{0:T(1024)} %param.6), kind=kLoop, calls=%fused_computation.16 | loop fusion | flops 3145728 | bytes 1067008 | tf_op jit(solution)/shard_map/and | solution.py:48
  54.9 20.7 %all-to-all-done = bf16[16,16,2048]{2,1,0:T(8,128)(2,1)S(1)} async-done(((bf16[16,16,2048]{2,1,0:T(8,128)(2,1)}), bf16[16,16,2048]{2,1,0:T(8,128)(2,1)S(1)}, u32[]{:S(2)}, u32[]{:S(2)}) %all-to-all-start) | async-done | bytes 1048608 | tf_op jit(solution)/shard_map/all_to_all | solution.py:41
  75.6 1.2 copy.19
  76.8 24.1 %all-gather.2.cloned.1.call-done = bf16[2,4096,256]{2,1,0:T(8,128)(2,1)} async-done(((bf16[2,256,256]{2,1,0:T(8,128)(2,1)}), bf16[2,4096,256]{2,1,0:T(8,128)(2,1)}) %all-gather.2.cloned.1.call-update) | async-done | bytes 4194320 | tf_op jit(solution)/shard_map/all_gather | solution.py:44
  100.9 3.8 %fusion.19 = (bf16[1,4096,256]{2,1,0:T(8,128)(2,1)}, bf16[1,4096,256]{2,1,0:T(8,128)(2,1)S(1)}) fusion(bf16[2,4096,256]{2,1,0:T(8,128)(2,1)} %all-gather.2.cloned.1.call-done), kind=kLoop, calls=%fused_computation.47 | loop fusion | bytes 8388608 | tf_op jit(solution)/shard_map/slice | solution.py:53
  104.7 4.1 %copy.8 = bf16[1,4096,256]{1,2,0:T(8,128)(2,1)} copy(bf16[1,4096,256]{2,1,0:T(8,128)(2,1)} %get-tuple-element.9) | data formatting | bytes 4194304 | tf_op jit(solution)/shard_map/slice | solution.py:53
  108.8 2.8 %copy.11 = bf16[1,4096,256]{1,2,0:T(8,128)(2,1)} copy(bf16[1,4096,256]{2,1,0:T(8,128)(2,1)S(1)} %get-tuple-element.10) | data formatting | bytes 4194304 | tf_op jit(solution)/shard_map/slice | solution.py:54
  111.7 0.0 copy-start.1
  111.7 26.9 %fusion = (f32[2,8,256]{2,1,0:T(8,128)S(1)}, f32[2,4096,256,8]{2,1,3,0:T(8,128)}) fusion(pred[256,4096]{0,1:T(8,128)(4,1)} %fusion.6, bf16[4096,2,128,1]{0,2,3,1:T(8,128)(2,1)} %bitcast.49, bf16[256,2,8,128]{3,2,1,0:T(8,128)(2,1)} %bitcast.50), kind=kOutput, calls=%fused_computation.9 | convolution fusion | flops 4345294848 | bytes 71319552 | tf_op jit(solution)/shard_map/qngd,knd->ngqk/dot_general | solution.py:56
  138.6 0.0 copy-done.1
  138.6 21.7 %fusion.1 = f32[2,8,256]{2,1,0:T(8,128)S(1)} fusion(f32[2,4096,256,8]{2,1,3,0:T(8,128)} %get-tuple-element.14, f32[2,8,256]{2,1,0:T(8,128)S(1)} %broadcast_maximum_fusion, pred[256,4096]{0,1:T(8,128)(4,1)S(1)} %copy-done.1), kind=kLoop, calls=%fused_computation.10 | loop fusion | flops 83881984 | bytes 68190208 | tf_op jit(solution)/shard_map/reduce_sum | solution.py:63
  160.3 25.7 %fusion.7 = bf16[256,2,8,128]{0,3,2,1:T(8,128)(2,1)S(1)} fusion(bf16[4096,2,128,1]{0,2,3,1:T(8,128)(2,1)} %bitcast.48, f32[2,4096,256,8]{2,1,3,0:T(8,128)} %get-tuple-element.14, f32[2,8,256]{2,1,0:T(8,128)S(1)} %broadcast_maximum_fusion, pred[256,4096]{0,1:T(8,128)(4,1)S(1)} %copy-done.1, f32[256,2,8]{0,2,1:T(8,128)S(1)} %bitcast.52), kind=kOutput, calls=%fused_computation.18 | convolution fusion | flops 4379901952 | bytes 71335936 | tf_op jit(solution)/shard_map/ngqk,knd->ngqd/dot_general | solution.py:64
  186.1 0.6 copy.13
  186.7 2.6 %scatter_custom_fusion.1 = bf16[256,2048]{1,0:T(8,128)(2,1)S(1)} fusion(s32[256]{0:T(256)S(1)} %get-tuple-element.12, bf16[256,2048]{1,0:T(8,128)(2,1)S(1)} %copy.13, bf16[]{:T(256)} %constant.19.clone.1), kind=kCustom, calls=%fused_computation.21 | custom fusion | bytes 1048578 | tf_op jit(solution)/shard_map/scatter | solution.py:71
  189.3 16.4 %convolution_convert_fusion = bf16[256,8192]{1,0:T(8,128)(2,1)} fusion(bf16[256,2048]{1,0:T(8,128)(2,1)S(1)} %scatter_custom_fusion.1, bf16[2048,8192]{1,0:T(8,128)(2,1)} %param.11), kind=kOutput, calls=%fused_computation.14 | convolution fusion | flops 8592031744 | bytes 38797312 | tf_op jit(solution)/shard_map/dot_general | solution.py:73
  205.8 0.0 reduce-scatter.2.cloned.1.call-update
  205.8 13.6 %reduce-scatter.2.cloned.1.call-done = bf16[128,8192]{1,0:T(8,128)(2,1)} async-done(((bf16[256,8192]{1,0:T(8,128)(2,1)}), bf16[128,8192]{1,0:T(8,128)(2,1)}) %reduce-scatter.2.cloned.1.call-update) | async-done | bytes 2097168 | tf_op jit(solution)/shard_map/reduce_scatter | solution.py:72
  (15 shorter events, 0.1 us)
Async XLA Ops:
  6.5 26.8 %copy-start = (bf16[256,2048]{1,0:T(8,128)(2,1)S(1)}, bf16[256,2048]{1,0:T(8,128)(2,1)}, u32[]{:S(2)}) copy-start(bf16[256,2048]{1,0:T(8,128)(2,1)} %param.8) | copy-start | bytes 3145732
  6.5 94.4 %all-gather.2.cloned.1.call-start = ((), (), s32[]{:S(2)}) async-start(), calls=%async_computation.2 | async-start | bytes 4456448 | tf_op jit(solution)/shard_map/all_gather | solution.py:44
  35.7 39.9 %all-to-all-start = ((bf16[16,16,2048]{2,1,0:T(8,128)(2,1)}), bf16[16,16,2048]{2,1,0:T(8,128)(2,1)S(1)}, u32[]{:S(2)}, u32[]{:S(2)}) async-start(bf16[16,16,2048]{2,1,0:T(8,128)(2,1)} %bitcast.7), calls=%async_computation | async-start | bytes 2097152 | tf_op jit(solution)/shard_map/all_to_all | solution.py:41
  42.3 177.1 %reduce-scatter.2.cloned.1.call-start = ((), (), s32[]{:S(2)}) async-start(), calls=%async_computation.3 | async-start | bytes 6291456 | tf_op jit(solution)/shard_map/reduce_scatter | solution.py:72
  111.7 26.9 %copy-start.1 = (pred[256,4096]{0,1:T(8,128)(4,1)S(1)}, pred[256,4096]{0,1:T(8,128)(4,1)}, u32[]{:S(2)}) copy-start(pred[256,4096]{0,1:T(8,128)(4,1)} %fusion.6) | copy-start | bytes 3145732
Sparse Core Ops, SparseCore 0:
  12.3 88.5 all-gather.1
  205.9 13.4 reduce-scatter.1
where the time goes:
time: 228 us; the launch traced here: 226 us
  matrix products  69.1 us (30%)
  waiting for transfers between devices  58.4 us (26%)
  local copies, waits for them, and re-layouts  40.7 us (18%)
  other arithmetic  33 us (14%)
  between operations  13.5 us (6%)
  starting transfers between devices  6.62 us (3%)
  blocking collectives  4.83 us (2%)
    dot_general x1, matrix products, shards(): jnp.einsum('qngd,knd->ngqk', query_split, key_split, preferred_element_ty...  26.9 us
    dot_general x1, matrix products, shards(): jnp.einsum('ngqk,knd->ngqd', expo.astype(jnp.bfloat16), value_split, pref...  25.7 us
    all_gather x1, waiting for transfers between devices, shards(): pieces = lax.all_gather(own_pair, 'seq', axis=1, tiled=True)  24.1 us
    reduce_sum x1, other arithmetic, shards(): denom = jnp.sum(expo, axis=-1)  21.7 us
    all_to_all x1, waiting for transfers between devices, shards(): lax.all_to_all(queries[send_order], 'seq', split_axis=0, concat_axis=0, t...  20.7 us
    dot_general x1, matrix products, shards(): jnp.dot(attn_new, out_weight, preferred_element_type=jnp.float32)  16.4 us
    scatter x1, local copies, waits for them, and re-layouts, shards(): inverse = jnp.zeros((total_rows,), jnp.int32).at[relayout].set(jnp.arange...  15.5 us
    reduce_scatter x1, waiting for transfers between devices, shards(): lax.psum_scatter(jnp.dot(attn_new, out_weight, preferred_element_type=jnp...  13.6 us
  transfers between devices with their start and end apart: 3, of which 3 were waited for; matrix products, arithmetic and copies ran while one was open for 16% of the time, Pallas kernels for 0%

commit v1 on v0

--- a/solution.py
+++ b/solution.py
@@ -1,11 +1,310 @@
+import functools
+
 import jax
 import jax.numpy as jnp
 from jax import lax
+from jax.experimental import pallas as pl
+from jax.experimental.pallas import tpu as pltpu
 from jax.sharding import PartitionSpec as P
 
 QH = 32
 KVH = 4
 HD = 128
+LONGEST_SHARE = 4
+MESH = pl.DeviceIdType.MESH
+WIDE = 512
+PIECES = 8
+
+
+def dot(a, b):
+    return jnp.dot(a, b, preferred_element_type=jnp.float32)
+
+
+def dot_nt(a, b):
+    return lax.dot_general(a, b, (((1,), (1,)), ((), ())), preferred_element_type=jnp.float32)
+
+
+def loop(low, high, body):
+    def step(i, carry):
+        body(i)
+        return carry
+
+    lax.fori_loop(low, high, step, 0)
+
+
+def fused_kernel(
+    n, reach, seg_ref, lay_ref, q_ref, k_ref, v_ref, w_hbm, out_ref,
+    kv, stage, bias, send_perm, recv_perm, rank_ref, mixed, sendb, arr, acc, part, other, wbuf,
+    w_sem, pair_send, pair_recv, far_send, far_recv, near_send, near_recv,
+    a2a_send, a2a_recv, sum_send, sum_recv,
+):
+    s = lax.axis_index("seq")
+    t = lax.axis_index("tp")
+    rows = q_ref.shape[0]
+    half = rows // 2
+    per_pair = rows // n
+    shared = kv.shape[1]
+    per_shared = q_ref.shape[1] // HD // shared
+    depth = per_shared * HD
+    wide_count = acc.shape[0]
+    w_rows = w_hbm.shape[0] // PIECES
+    place = lax.rem(s, reach)
+    base = s - place
+
+    def w_copy(i):
+        cut = pl.ds(pl.multiple_of(i * w_rows, w_rows), w_rows)
+        return pltpu.make_async_copy(w_hbm.at[cut], wbuf.at[cut], w_sem.at[i])
+
+    loop(0, PIECES, lambda i: w_copy(i).start())
+
+    own_half = pl.ds(pl.multiple_of(t * half, half), half)
+    other_half = pl.ds(pl.multiple_of((1 - t) * half, half), half)
+    for g in range(shared):
+        mine = pl.ds(pl.multiple_of((t * shared + g) * HD, HD), HD)
+        theirs = pl.ds(pl.multiple_of(((1 - t) * shared + g) * HD, HD), HD)
+        kv[0, g, own_half, 0:HD] = k_ref[:, mine]
+        kv[0, g, own_half, HD : 2 * HD] = v_ref[:, mine]
+        stage[g, :, 0:HD] = k_ref[:, theirs]
+        stage[g, :, HD : 2 * HD] = v_ref[:, theirs]
+
+    barrier = pltpu.get_barrier_semaphore()
+    loop(
+        1, n,
+        lambda e: pl.semaphore_signal(
+            barrier, inc=1, device_id={"seq": lax.rem(s + e, n)}, device_id_type=MESH
+        ),
+    )
+    pl.semaphore_signal(barrier, inc=1, device_id={"tp": 1 - t}, device_id_type=MESH)
+    pl.semaphore_wait(barrier, n)
+
+    def pair_copy(g):
+        return pltpu.make_async_remote_copy(
+            src_ref=stage.at[g], dst_ref=kv.at[0, g, own_half],
+            send_sem=pair_send.at[g], recv_sem=pair_recv.at[g],
+            device_id={"tp": 1 - t}, device_id_type=MESH,
+        )
+
+    def far_copy(g):
+        return pltpu.make_async_remote_copy(
+            src_ref=kv.at[0, g], dst_ref=kv.at[reach, g],
+            send_sem=far_send.at[g], recv_sem=far_recv.at[g],
+            device_id={"seq": lax.rem(s + reach, n)}, device_id_type=MESH,
+        )
+
+    def near_copy(g, e, slot):
+        return pltpu.make_async_remote_copy(
+            src_ref=kv.at[slot, g], dst_ref=kv.at[e, g],
+            send_sem=near_send.at[g, e], recv_sem=near_recv.at[g, e],
+            device_id={"seq": base + lax.rem(place + e, reach)}, device_id_type=MESH,
+        )
+
+    def own_out(g):
+        pair_copy(g).wait_recv()
+
+        @pl.when(s + reach < n)
+        def _():
+            far_copy(g).start()
+
+        for e in range(1, reach):
+
+            @pl.when(place + e < reach)
+            def _():
+                near_copy(g, e, 0).start()
+
+    def relay(g):
+        @pl.when(s >= reach)
+        def _():
+            far_copy(g).wait_recv()
+            for e in range(1, reach):
+
+                @pl.when(place + e >= reach)
+                def _():
+                    near_copy(g, e, reach).start()
+
+    for g in range(shared):
+        pair_copy(g).start()
+    for e in range(1, reach + 1):
+
+        @pl.when(s < e)
+        def _():
+            kv[e] = jnp.zeros_like(kv[e])
+
+    own_out(0)
+
+    row_id = lax.broadcasted_iota(jnp.int32, (rows, rows), 0)
+    col_id = lax.broadcasted_iota(jnp.int32, (rows, rows), 1)
+    query_seg = jnp.broadcast_to(seg_ref[pl.ds(s, 1), :], (rows, rows)).T
+    for d in range(reach + 1):
+        key_seg = seg_ref[pl.ds(jnp.maximum(s - d, 0), 1), :]
+        live = query_seg == jnp.where(s >= d, key_seg, -1)
+        if d == 0:
+            live = live & (col_id <= row_id)
+        bias[d] = jnp.where(live, jnp.float32(0.0), jnp.float32(-1e30))
+
+    relay(0)
+    for g in range(1, shared):
+        own_out(g)
+
+    before = jnp.where(row_id < col_id, 1.0, 0.0).astype(jnp.bfloat16)
+    local = lay_ref[...] - s * rows
+    is_mine = (local >= 0) & (local < rows)
+    ranks = dot(jnp.where(is_mine, 1.0, 0.0).astype(jnp.bfloat16), before)
+    rank_ref[...] = jnp.where(is_mine, ranks, -1.0)
+    rank_id = lax.broadcasted_iota(jnp.int32, (per_pair, rows), 0).astype(jnp.float32)
+
+    def one_target(b):
+        pick = jnp.where(rank_ref[pl.ds(b, 1), :] == rank_id, 1.0, 0.0).astype(jnp.bfloat16)
+        token = jnp.where(lay_ref[pl.ds(b, 1), :] - s * rows == row_id, 1.0, 0.0).astype(jnp.bfloat16)
+        cut = pl.ds(pl.multiple_of(b * per_pair, per_pair), per_pair)
+        send_perm[cut, :] = dot_nt(pick, token).astype(jnp.bfloat16)
+
+    loop(0, n, one_target)
+    origin = lay_ref[pl.ds(s, 1), :] // rows
+    block_id = lax.broadcasted_iota(jnp.int32, (n, rows), 0)
+    from_block = jnp.where(origin == block_id, 1.0, 0.0)
+    earlier = dot(from_block.astype(jnp.bfloat16), before)
+    rank = jnp.sum(from_block * earlier, axis=0, keepdims=True)
+    slot_of = origin.astype(jnp.float32) * per_pair + rank
+    slot_col = jnp.broadcast_to(slot_of, (rows, rows)).T
+    recv_perm[...] = jnp.where(slot_col == col_id.astype(jnp.float32), 1.0, 0.0).astype(jnp.bfloat16)
+
+    for g in range(1, shared):
+        relay(g)
+
+    def a2a_copy(g, e):
+        target = lax.rem(s + e, n)
+        return pltpu.make_async_remote_copy(
+            src_ref=sendb.at[g, pl.ds(pl.multiple_of(target * per_pair, per_pair), per_pair)],
+            dst_ref=arr.at[g, pl.ds(pl.multiple_of(s * per_pair, per_pair), per_pair)],
+            send_sem=a2a_send.at[g, e], recv_sem=a2a_recv.at[g, e],
+            device_id={"seq": target}, device_id_type=MESH,
+        )
+
+    factor = HD ** (-0.5) * 1.4426950408889634
+
+    for g in range(shared):
+        for e in range(1, reach):
+
+            @pl.when(s >= e)
+            def _():
+                near_copy(g, e, 0).wait_recv()
+
+        def one_head(h):
+            q = q_ref[:, pl.ds(pl.multiple_of((g * per_shared + h) * HD, HD), HD)]
+            scores = [dot_nt(q, kv[d, g, :, 0:HD]) + bias[d] for d in range(reach + 1)]
+            peak = jnp.max(functools.reduce(jnp.maximum, scores), axis=1, keepdims=True)
+            expo = [jnp.exp2((x - peak) * factor) for x in scores]
+            denom = jnp.sum(functools.reduce(jnp.add, expo), axis=1, keepdims=True)
+            update = functools.reduce(
+                jnp.add,
+                [dot(x.astype(jnp.bfloat16), kv[d, g, :, HD : 2 * HD]) for d, x in enumerate(expo)],
+            )
+            attn = (update / denom).astype(jnp.bfloat16)
+            sendb[g, :, pl.ds(pl.multiple_of(h * HD, HD), HD)] = dot(
+                send_perm[...], attn
+            ).astype(jnp.bfloat16)
+
+        loop(0, per_shared, one_head)
+        loop(1, n, lambda e: a2a_copy(g, e).start())
+        keep = pl.ds(pl.multiple_of(s * per_pair, per_pair), per_pair)
+        arr[g, keep, :] = sendb[g, keep, :]
+
+    def sum_copy(c):
+        return pltpu.make_async_remote_copy(
+            src_ref=part.at[c, other_half], dst_ref=other.at[c],
+            send_sem=sum_send.at[c], recv_sem=sum_recv.at[c],
+            device_id={"tp": 1 - t}, device_id_type=MESH,
+        )
+
+    for g in range(shared):
+        share = PIECES // shared
+        loop(g * share, (g + 1) * share, lambda i: w_copy(i).wait())
+        loop(1, n, lambda e: a2a_copy(g, e).wait_recv())
+        mixed[...] = dot(recv_perm[...], arr[g]).astype(jnp.bfloat16)
+
+        def one_width(c):
+            cut = pl.ds(pl.multiple_of(c * WIDE, WIDE), WIDE)
+            term = dot(mixed[...], wbuf[g * depth : (g + 1) * depth, cut])
+            if g > 0:
+                term = term + acc[c]
+            if g < shared - 1:
+                acc[c] = term
+            else:
+                part[c] = term.astype(jnp.bfloat16)
+                sum_copy(c).start()
+
+        loop(0, wide_count, one_width)
+
+    def finish(c):
+        sum_copy(c).wait_recv()
+        total = part[c, own_half, :].astype(jnp.float32) + other[c].astype(jnp.float32)
+        out_ref[:, pl.ds(pl.multiple_of(c * WIDE, WIDE), WIDE)] = total.astype(jnp.bfloat16)
+
+    loop(0, wide_count, finish)
+
+    for g in range(shared):
+        pair_copy(g).wait_send()
+
+        @pl.when(s + reach < n)
+        def _():
+            far_copy(g).wait_send()
+
+        for e in range(1, reach):
+
+            @pl.when((place + e < reach) | (s >= reach))
+            def _():
+                near_copy(g, e, 0).wait_send()
+
+        loop(1, n, lambda e: a2a_copy(g, e).wait_send())
+    loop(0, wide_count, lambda c: sum_copy(c).wait_send())
+
+
+def fused_shards(segment_ids, relayout, queries, keys, values, out_weight):
+    n = lax.axis_size("seq")
+    rows = queries.shape[0]
+    reach = n // LONGEST_SHARE
+    shared = keys.shape[1] // HD // 2
+    depth = queries.shape[1] // shared
+    width = out_weight.shape[1]
+    wide_count = width // WIDE
+    bf16, f32 = jnp.bfloat16, jnp.float32
+    dma = pltpu.SemaphoreType.DMA
+    vmem = pl.BlockSpec(memory_space=pltpu.VMEM)
+    return pl.pallas_call(
+        functools.partial(fused_kernel, n, reach),
+        out_shape=jax.ShapeDtypeStruct((rows // 2, width), bf16),
+        in_specs=[vmem] * 5 + [pl.BlockSpec(memory_space=pl.ANY)],
+        out_specs=vmem,
+        scratch_shapes=[
+            pltpu.VMEM((reach + 1, shared, rows, 2 * HD), bf16),
+            pltpu.VMEM((shared, rows // 2, 2 * HD), bf16),
+            pltpu.VMEM((reach + 1, rows, rows), f32),
+            pltpu.VMEM((rows, rows), bf16),
+            pltpu.VMEM((rows, rows), bf16),
+            pltpu.VMEM((n, rows), f32),
+            pltpu.VMEM((rows, depth), bf16),
+            pltpu.VMEM((shared, rows, depth), bf16),
+            pltpu.VMEM((shared, rows, depth), bf16),
+            pltpu.VMEM((wide_count, rows, WIDE), f32),
+            pltpu.VMEM((wide_count, rows, WIDE), bf16),
+            pltpu.VMEM((wide_count, rows // 2, WIDE), bf16),
+            pltpu.VMEM(out_weight.shape, bf16),
+            dma((PIECES,)),
+            dma((shared,)),
+            dma((shared,)),
+            dma((shared,)),
+            dma((shared,)),
+            dma((shared, reach)),
+            dma((shared, reach)),
+            dma((shared, n)),
+            dma((shared, n)),
+            dma((wide_count,)),
+            dma((wide_count,)),
+        ],
+        compiler_params=pltpu.CompilerParams(
+            collective_id=0, has_side_effects=True, vmem_limit_bytes=63 * 1024 * 1024
+        ),
+    )(segment_ids.reshape(n, rows), relayout.reshape(n, rows), queries, keys, values, out_weight)
 
 
 def shards(segment_ids, relayout, queries, keys, values, out_weight):
@@ -79,7 +378,7 @@
 
 def solution(mesh):
     return jax.shard_map(
-        shards,
+        fused_shards if mesh.shape["tp"] == 2 else shards,
         mesh=mesh,
         in_specs=(
             P(),

time: 228 us -> 71.1 us (0.31)
  matrix products: 69.1 us -> 0 us
  Pallas kernels: 0 us -> 65.1 us
  waiting for transfers between devices: 58.4 us -> 0 us
  local copies, waits for them, and re-layouts: 40.7 us -> 5.74 us
  other arithmetic: 33 us -> 0 us
  between operations: 13.5 us -> 0.01 us
  starting transfers between devices: 6.62 us -> 0 us
  blocking collectives: 4.83 us -> 0 us
    dot_general x3 -> x0, matrix products: 69.1 us -> none  [the longest x1 26.9 us: shards(): jnp.einsum('qngd,knd->ngqk', query_split, key_split, preferred_element_ty...]
    pallas_call x0 -> x1, Pallas kernels: none -> 65.1 us  [fused_shards(): pl.pallas_call(functools.partial(fused_kernel, n, reach), out_shape=jax.S...]
    all_gather x1 -> x0, waiting for transfers between devices: 24.1 us -> none  [shards(): pieces = lax.all_gather(own_pair, 'seq', axis=1, tiled=True)]
    reduce_sum x1 -> x0, other arithmetic: 21.7 us -> none  [shards(): denom = jnp.sum(expo, axis=-1)]
    all_to_all x1 -> x0, waiting for transfers between devices: 20.7 us -> none  [shards(): lax.all_to_all(queries[send_order], 'seq', split_axis=0, concat_axis=0, t...]
    scatter x2 -> x0, local copies, waits for them, and re-layouts: 18.1 us -> none  [the longest x1 15.5 us: shards(): inverse = jnp.zeros((total_rows,), jnp.int32).at[relayout].set(jnp.arange...]
    reduce_scatter x1 -> x0, waiting for transfers between devices: 13.6 us -> none  [shards(): lax.psum_scatter(jnp.dot(attn_new, out_weight, preferred_element_type=jnp...]
    slice x3 -> x0, local copies, waits for them, and re-layouts: 10.8 us -> none  [the longest x2 7.93 us: shards(): key_split = pieces[0].reshape(count, shared_here, HD)]
  transfers between devices with their start and end apart: 3 -> 0, of which waited for: 3 -> 0; matrix products, arithmetic and copies ran while one was open for 16% -> 0% of each run, Pallas kernels for 0% -> 0%
where the time goes in v1:
time: 71.1 us; the launch traced here: 70.8 us
  Pallas kernels  65.1 us (92%)
  local copies, waits for them, and re-layouts  5.74 us (8%)
    pallas_call x1, Pallas kernels, fused_shards(): pl.pallas_call(functools.partial(fused_kernel, n, reach), out_shape=jax.S...  65.1 us
    unnamed x1, local copies, waits for them, and re-layouts  3.1 us

profile of v1, /device:TPU:15, one launch (start us, length us, event | category | flops | bytes accessed | tf_op | source)
XLA Modules:
  0.0 70.8 jit_solution(15568080811063622869)
XLA Ops:
  0.0 1.3 %reshape.6.seg_ref = s32[16,256]{1,0:T(8,128)} reshape(s32[4096]{0:T(1024)} %param.6) | data formatting | bytes 32768 | tf_op jit(solution)/shard_map/reshape | solution.py:307
  1.3 1.3 %reshape.7.lay_ref = s32[16,256]{1,0:T(8,128)} reshape(s32[4096]{0:T(1024)} %param.7) | data formatting | bytes 32768 | tf_op jit(solution)/shard_map/reshape | solution.py:307
  2.6 65.1 %shard_map.64 = bf16[128,8192]{1,0:T(8,128)(2,1)} custom-call(s32[16,256]{1,0:T(8,128)} %reshape.6.seg_ref, s32[16,256]{1,0:T(8,128)} %reshape.7.lay_ref, bf16[256,2048]{1,0:T(8,128)(2,1)} %q_ref.1, bf16[128,512]{1,0:T(8,128)(2,1)} %k_ref.1, bf16[128,512]{1,0:T(8,128)(2,1)} %v_ref.1, bf16[2048,8192]{1,0:T(8,128)(2,1)} %w_hbm.1), custom_call_target="tpu_custom_call" | custom-call | tf_op jit(solution)/shard_map/pallas_call | solution.py:273
  67.7 3.1 %copy.8 = bf16[128,8192]{1,0:T(8,128)(2,1)} copy(bf16[128,8192]{1,0:T(8,128)(2,1)} %shard_map.64) | data formatting | bytes 4194304

commit v2 on v1

--- a/solution.py
+++ b/solution.py
@@ -14,6 +14,8 @@
 MESH = pl.DeviceIdType.MESH
 WIDE = 512
 PIECES = 8
+CUTS = 4
+TOGETHER = 2
 
 
 def dot(a, b):
@@ -33,10 +35,11 @@
 
 
 def fused_kernel(
-    n, reach, seg_ref, lay_ref, q_ref, k_ref, v_ref, w_hbm, out_ref,
-    kv, stage, bias, send_perm, recv_perm, rank_ref, mixed, sendb, arr, acc, part, other, wbuf,
+    n, reach, seg_in, lay_in, q_ref, k_ref, v_ref, w_hbm, own_out_ref, other_ref,
+    seg_ref, lay_ref, kv, stage, key_tag, query_tag, own_first, send_perm, recv_perm, rank_ref, q_sorted,
+    mixed, sendb, arr, acc, part, wbuf,
     w_sem, pair_send, pair_recv, far_send, far_recv, near_send, near_recv,
-    a2a_send, a2a_recv, sum_send, sum_recv,
+    a2a_send, a2a_recv, sum_send, sum_recv, keep_sem,
 ):
     s = lax.axis_index("seq")
     t = lax.axis_index("tp")
@@ -45,11 +48,21 @@
     per_pair = rows // n
     shared = kv.shape[1]
     per_shared = q_ref.shape[1] // HD // shared
-    depth = per_shared * HD
+    cuts, _, depth = sendb.shape
+    cut_heads = depth // HD
     wide_count = acc.shape[0]
     w_rows = w_hbm.shape[0] // PIECES
     place = lax.rem(s, reach)
     base = s - place
+
+    barrier = pltpu.get_barrier_semaphore()
+    loop(
+        1, n,
+        lambda e: pl.semaphore_signal(
+            barrier, inc=1, device_id={"seq": lax.rem(s + e, n)}, device_id_type=MESH
+        ),
+    )
+    pl.semaphore_signal(barrier, inc=1, device_id={"tp": 1 - t}, device_id_type=MESH)
 
     def w_copy(i):
         cut = pl.ds(pl.multiple_of(i * w_rows, w_rows), w_rows)
@@ -67,14 +80,6 @@
         stage[g, :, 0:HD] = k_ref[:, theirs]
         stage[g, :, HD : 2 * HD] = v_ref[:, theirs]
 
-    barrier = pltpu.get_barrier_semaphore()
-    loop(
-        1, n,
-        lambda e: pl.semaphore_signal(
-            barrier, inc=1, device_id={"seq": lax.rem(s + e, n)}, device_id_type=MESH
-        ),
-    )
-    pl.semaphore_signal(barrier, inc=1, device_id={"tp": 1 - t}, device_id_type=MESH)
     pl.semaphore_wait(barrier, n)
 
     def pair_copy(g):
@@ -131,19 +136,23 @@
 
     own_out(0)
 
-    row_id = lax.broadcasted_iota(jnp.int32, (rows, rows), 0)
-    col_id = lax.broadcasted_iota(jnp.int32, (rows, rows), 1)
-    query_seg = jnp.broadcast_to(seg_ref[pl.ds(s, 1), :], (rows, rows)).T
+    lines = rows // 128
+    for ref, source in ((seg_ref, seg_in), (lay_ref, lay_in)):
+        for i in range(lines):
+            ref[:, i * 128 : (i + 1) * 128] = source[pl.ds(i, n, stride=lines), :]
+
+    tag_id = lax.broadcasted_iota(jnp.int32, (rows, HD), 1)
     for d in range(reach + 1):
-        key_seg = seg_ref[pl.ds(jnp.maximum(s - d, 0), 1), :]
-        live = query_seg == jnp.where(s >= d, key_seg, -1)
-        if d == 0:
-            live = live & (col_id <= row_id)
-        bias[d] = jnp.where(live, jnp.float32(0.0), jnp.float32(-1e30))
+        key_seg = jnp.where(s >= d, seg_ref[pl.ds(jnp.maximum(s - d, 0), 1), :], HD - 1)
+        key_col = jnp.broadcast_to(key_seg, (HD, rows)).T
+        key_tag[d] = jnp.where(key_col == tag_id, 1.0, 0.0).astype(jnp.bfloat16)
 
     relay(0)
     for g in range(1, shared):
         own_out(g)
+
+    row_id = lax.broadcasted_iota(jnp.int32, (rows, rows), 0)
+    col_id = lax.broadcasted_iota(jnp.int32, (rows, rows), 1)
 
     before = jnp.where(row_id < col_id, 1.0, 0.0).astype(jnp.bfloat16)
     local = lay_ref[...] - s * rows
@@ -159,6 +168,18 @@
         send_perm[cut, :] = dot_nt(pick, token).astype(jnp.bfloat16)
 
     loop(0, n, one_target)
+
+    def sort_queries(c):
+        cut = pl.ds(pl.multiple_of(c * depth, depth), depth)
+        q_sorted[:, cut] = dot(send_perm[...], q_ref[:, cut]).astype(jnp.bfloat16)
+
+    loop(0, cuts, sort_queries)
+    chosen = send_perm[...].astype(jnp.float32)
+    position = jnp.sum(chosen * col_id.astype(jnp.float32), axis=1, keepdims=True)
+    document = jnp.sum(chosen * seg_ref[pl.ds(s, 1), :].astype(jnp.float32), axis=1, keepdims=True)
+    query_tag[...] = jnp.where(document == tag_id.astype(jnp.float32), 0.0, -1e30).astype(jnp.bfloat16)
+    own_first[...] = jnp.where(col_id.astype(jnp.float32) <= position, 1.0, 0.0)
+
     origin = lay_ref[pl.ds(s, 1), :] // rows
     block_id = lax.broadcasted_iota(jnp.int32, (n, rows), 0)
     from_block = jnp.where(origin == block_id, 1.0, 0.0)
@@ -182,63 +203,85 @@
 
     factor = HD ** (-0.5) * 1.4426950408889634
 
-    for g in range(shared):
-        for e in range(1, reach):
-
-            @pl.when(s >= e)
-            def _():
-                near_copy(g, e, 0).wait_recv()
-
-        def one_head(h):
-            q = q_ref[:, pl.ds(pl.multiple_of((g * per_shared + h) * HD, HD), HD)]
-            scores = [dot_nt(q, kv[d, g, :, 0:HD]) + bias[d] for d in range(reach + 1)]
-            peak = jnp.max(functools.reduce(jnp.maximum, scores), axis=1, keepdims=True)
-            expo = [jnp.exp2((x - peak) * factor) for x in scores]
-            denom = jnp.sum(functools.reduce(jnp.add, expo), axis=1, keepdims=True)
-            update = functools.reduce(
-                jnp.add,
-                [dot(x.astype(jnp.bfloat16), kv[d, g, :, HD : 2 * HD]) for d, x in enumerate(expo)],
-            )
-            attn = (update / denom).astype(jnp.bfloat16)
-            sendb[g, :, pl.ds(pl.multiple_of(h * HD, HD), HD)] = dot(
-                send_perm[...], attn
-            ).astype(jnp.bfloat16)
-
-        loop(0, per_shared, one_head)
-        loop(1, n, lambda e: a2a_copy(g, e).start())
+    ones = jnp.ones((rows, HD), jnp.bfloat16)
+
+    def one_head(g, h, to):
+        q = q_sorted[:, pl.ds(pl.multiple_of(h * HD, HD), HD)]
+        q = jnp.concatenate([q, query_tag[...]], axis=1)
+        scores = [
+            dot_nt(q, jnp.concatenate([kv[d, g, :, 0:HD], key_tag[d]], axis=1)) for d in range(reach + 1)
+        ]
+        is_own = own_first[...] > 0.5
+        scores = [jnp.where(is_own, scores[0], scores[reach])] + scores[1:reach]
+        peak = jnp.max(functools.reduce(jnp.maximum, scores), axis=1, keepdims=True)
+        expo = [jnp.exp2((x - peak) * factor) for x in scores]
+        expo = (
+            [jnp.where(is_own, expo[0], 0.0)] + expo[1:] + [jnp.where(is_own, 0.0, expo[0])]
+        )
+        update = functools.reduce(
+            jnp.add,
+            [
+                dot(x.astype(jnp.bfloat16), jnp.concatenate([kv[d, g, :, HD : 2 * HD], ones], axis=1))
+                for d, x in enumerate(expo)
+            ],
+        )
+        sendb[to, :, pl.ds(pl.multiple_of((h - to * cut_heads) * HD, HD), HD)] = (
+            update[:, 0:HD] / update[:, HD : 2 * HD]
+        ).astype(jnp.bfloat16)
+
+    for c in range(cuts):
+        g = c * cut_heads // per_shared
+        if c * cut_heads % per_shared == 0:
+            for e in range(1, reach):
+
+                @pl.when(s >= e)
+                def _():
+                    near_copy(g, e, 0).wait_recv()
+
+        def heads(i):
+            for k in range(TOGETHER):
+                one_head(g, c * cut_heads + i * TOGETHER + k, c)
+
+        loop(0, cut_heads // TOGETHER, heads)
+        loop(1, n, lambda e: a2a_copy(c, e).start())
         keep = pl.ds(pl.multiple_of(s * per_pair, per_pair), per_pair)
-        arr[g, keep, :] = sendb[g, keep, :]
+        arr[c, keep, :] = sendb[c, keep, :]
+
+    def wide_cut(c):
+        return pl.ds(pl.multiple_of(c * WIDE, WIDE), WIDE)
 
     def sum_copy(c):
         return pltpu.make_async_remote_copy(
-            src_ref=part.at[c, other_half], dst_ref=other.at[c],
+            src_ref=part.at[c, other_half], dst_ref=other_ref.at[:, wide_cut(c)],
             send_sem=sum_send.at[c], recv_sem=sum_recv.at[c],
             device_id={"tp": 1 - t}, device_id_type=MESH,
         )
 
-    for g in range(shared):
-        share = PIECES // shared
+    def keep_copy(c):
+        return pltpu.make_async_copy(part.at[c, own_half], own_out_ref.at[:, wide_cut(c)], keep_sem.at[c])
+
+    for g in range(cuts):
+        share = PIECES // cuts
         loop(g * share, (g + 1) * share, lambda i: w_copy(i).wait())
         loop(1, n, lambda e: a2a_copy(g, e).wait_recv())
         mixed[...] = dot(recv_perm[...], arr[g]).astype(jnp.bfloat16)
 
         def one_width(c):
-            cut = pl.ds(pl.multiple_of(c * WIDE, WIDE), WIDE)
-            term = dot(mixed[...], wbuf[g * depth : (g + 1) * depth, cut])
+            term = dot(mixed[...], wbuf[g * depth : (g + 1) * depth, wide_cut(c)])
             if g > 0:
                 term = term + acc[c]
-            if g < shared - 1:
+            if g < cuts - 1:
                 acc[c] = term
             else:
                 part[c] = term.astype(jnp.bfloat16)
                 sum_copy(c).start()
+                keep_copy(c).start()
 
         loop(0, wide_count, one_width)
 
     def finish(c):
+        keep_copy(c).wait()
         sum_copy(c).wait_recv()
-        total = part[c, own_half, :].astype(jnp.float32) + other[c].astype(jnp.float32)
-        out_ref[:, pl.ds(pl.multiple_of(c * WIDE, WIDE), WIDE)] = total.astype(jnp.bfloat16)
 
     loop(0, wide_count, finish)
 
@@ -255,7 +298,8 @@
             def _():
                 near_copy(g, e, 0).wait_send()
 
-        loop(1, n, lambda e: a2a_copy(g, e).wait_send())
+    for c in range(cuts):
+        loop(1, n, lambda e: a2a_copy(c, e).wait_send())
     loop(0, wide_count, lambda c: sum_copy(c).wait_send())
 
 
@@ -264,30 +308,34 @@
     rows = queries.shape[0]
     reach = n // LONGEST_SHARE
     shared = keys.shape[1] // HD // 2
-    depth = queries.shape[1] // shared
+    depth = queries.shape[1] // CUTS
     width = out_weight.shape[1]
     wide_count = width // WIDE
     bf16, f32 = jnp.bfloat16, jnp.float32
     dma = pltpu.SemaphoreType.DMA
     vmem = pl.BlockSpec(memory_space=pltpu.VMEM)
-    return pl.pallas_call(
+    own, other = pl.pallas_call(
         functools.partial(fused_kernel, n, reach),
-        out_shape=jax.ShapeDtypeStruct((rows // 2, width), bf16),
+        out_shape=[jax.ShapeDtypeStruct((rows // 2, width), bf16)] * 2,
         in_specs=[vmem] * 5 + [pl.BlockSpec(memory_space=pl.ANY)],
-        out_specs=vmem,
+        out_specs=[pl.BlockSpec(memory_space=pl.ANY)] * 2,
         scratch_shapes=[
+            pltpu.VMEM((n, rows), jnp.int32),
+            pltpu.VMEM((n, rows), jnp.int32),
             pltpu.VMEM((reach + 1, shared, rows, 2 * HD), bf16),
             pltpu.VMEM((shared, rows // 2, 2 * HD), bf16),
-            pltpu.VMEM((reach + 1, rows, rows), f32),
+            pltpu.VMEM((reach + 1, rows, HD), bf16),
+            pltpu.VMEM((rows, HD), bf16),
+            pltpu.VMEM((rows, rows), f32),
             pltpu.VMEM((rows, rows), bf16),
             pltpu.VMEM((rows, rows), bf16),
             pltpu.VMEM((n, rows), f32),
+            pltpu.VMEM(queries.shape, bf16),
             pltpu.VMEM((rows, depth), bf16),
-            pltpu.VMEM((shared, rows, depth), bf16),
-            pltpu.VMEM((shared, rows, depth), bf16),
+            pltpu.VMEM((CUTS, rows, depth), bf16),
+            pltpu.VMEM((CUTS, rows, depth), bf16),
             pltpu.VMEM((wide_count, rows, WIDE), f32),
             pltpu.VMEM((wide_count, rows, WIDE), bf16),
-            pltpu.VMEM((wide_count, rows // 2, WIDE), bf16),
             pltpu.VMEM(out_weight.shape, bf16),
             dma((PIECES,)),
             dma((shared,)),
@@ -296,15 +344,17 @@
             dma((shared,)),
             dma((shared, reach)),
             dma((shared, reach)),
-            dma((shared, n)),
-            dma((shared, n)),
+            dma((CUTS, n)),
+            dma((CUTS, n)),
+            dma((wide_count,)),
             dma((wide_count,)),
             dma((wide_count,)),
         ],
         compiler_params=pltpu.CompilerParams(
             collective_id=0, has_side_effects=True, vmem_limit_bytes=63 * 1024 * 1024
         ),
-    )(segment_ids.reshape(n, rows), relayout.reshape(n, rows), queries, keys, values, out_weight)
+    )(segment_ids.reshape(-1, 128), relayout.reshape(-1, 128), queries, keys, values, out_weight)
+    return (own.astype(f32) + other.astype(f32)).astype(bf16)
 
 
 def shards(segment_ids, relayout, queries, keys, values, out_weight):

time: 71.1 us -> 64.2 us (0.903)
  local copies, waits for them, and re-layouts: 5.74 us -> 0 us
  Pallas kernels: 65.1 us -> 60 us
  other arithmetic: 0 us -> 4.04 us
    pallas_call x1, Pallas kernels: 65.1 us -> 60 us  [fused_shards(): pl.pallas_call(functools.partial(fused_kernel, n, reach), out_shape=[jax....]
    convert_element_type x0 -> x1, other arithmetic: none -> 4.04 us  [fused_shards(): return (own.astype(f32) + other.astype(f32)).astype(bf16)]
    unnamed x1 -> x0, local copies, waits for them, and re-layouts: 3.1 us -> none
    reshape x2 -> x0, local copies, waits for them, and re-layouts: 2.64 us -> none  [the longest x1 1.33 us: fused_shards(): segment_ids.reshape(n, rows)]
where the time goes in v2:
time: 64.2 us; the launch traced here: 64 us
  Pallas kernels  60 us (93%)
  other arithmetic  4.04 us (6%)
    pallas_call x1, Pallas kernels, fused_shards(): pl.pallas_call(functools.partial(fused_kernel, n, reach), out_shape=[jax....  60 us
    convert_element_type x1, other arithmetic, fused_shards(): return (own.astype(f32) + other.astype(f32)).astype(bf16)  4.04 us

profile of v2, /device:TPU:15, one launch (start us, length us, event | category | flops | bytes accessed | tf_op | source)
XLA Modules:
  0.0 64.0 jit_solution(8168614651285359662)
XLA Ops:
  0.0 60.0 %shard_map.64 = (bf16[128,8192]{1,0:T(8,128)(2,1)}, bf16[128,8192]{1,0:T(8,128)(2,1)}) custom-call(s32[32,128]{1,0:T(8,128)} %bitcast.2, s32[32,128]{1,0:T(8,128)} %bitcast.3, bf16[256,2048]{1,0:T(8,128)(2,1)} %q_ref.1, bf16[128,512]{1,0:T(8,128)(2,1)} %k_ref.1, bf16[128,512]{1,0:T(8,128)(2,1)} %v_ref.1, bf16[2048,8192]{1,0:T(8,128)(2,1)} %w_hbm.1), custom_call_target="tpu_custom_call" | custom-call | tf_op jit(solution)/shard_map/pallas_call | solution.py:317
  60.0 4.0 %add_convert_fusion = bf16[128,8192]{1,0:T(8,128)(2,1)} fusion(bf16[128,8192]{1,0:T(8,128)(2,1)} %get-tuple-element.8, bf16[128,8192]{1,0:T(8,128)(2,1)} %get-tuple-element.7), kind=kLoop, calls=%fused_computation | loop fusion | flops 4194304 | bytes 6291456 | tf_op jit(solution)/shard_map/convert_element_type | solution.py:357

commit v3 on v2

--- a/solution.py
+++ b/solution.py
@@ -13,9 +13,11 @@
 LONGEST_SHARE = 4
 MESH = pl.DeviceIdType.MESH
 WIDE = 512
-PIECES = 8
+PIECES = 32
 CUTS = 4
 TOGETHER = 2
+BEHIND = 3
+COPIES = 8
 
 
 def dot(a, b):
@@ -35,9 +37,9 @@
 
 
 def fused_kernel(
-    n, reach, seg_in, lay_in, q_ref, k_ref, v_ref, w_hbm, own_out_ref, other_ref,
+    n, reach, seg_in, lay_in, q_ref, k_ref, v_ref, w_hbm, out_ref,
     seg_ref, lay_ref, kv, stage, key_tag, query_tag, own_first, send_perm, recv_perm, rank_ref, q_sorted,
-    mixed, sendb, arr, acc, part, wbuf,
+    mixed, sendb, arr, acc, part, other, wbuf,
     w_sem, pair_send, pair_recv, far_send, far_recv, near_send, near_recv,
     a2a_send, a2a_recv, sum_send, sum_recv, keep_sem,
 ):
@@ -68,8 +70,6 @@
         cut = pl.ds(pl.multiple_of(i * w_rows, w_rows), w_rows)
         return pltpu.make_async_copy(w_hbm.at[cut], wbuf.at[cut], w_sem.at[i])
 
-    loop(0, PIECES, lambda i: w_copy(i).start())
-
     own_half = pl.ds(pl.multiple_of(t * half, half), half)
     other_half = pl.ds(pl.multiple_of((1 - t) * half, half), half)
     for g in range(shared):
@@ -239,6 +239,9 @@
                     near_copy(g, e, 0).wait_recv()
 
         def heads(i):
+            w_step = PIECES * TOGETHER // (cuts * cut_heads)
+            first = (c * cut_heads // TOGETHER + i) * w_step
+            loop(first, first + w_step, lambda j: w_copy(j).start())
             for k in range(TOGETHER):
                 one_head(g, c * cut_heads + i * TOGETHER + k, c)
 
@@ -252,13 +255,19 @@
 
     def sum_copy(c):
         return pltpu.make_async_remote_copy(
-            src_ref=part.at[c, other_half], dst_ref=other_ref.at[:, wide_cut(c)],
+            src_ref=part.at[c, other_half], dst_ref=other.at[c],
             send_sem=sum_send.at[c], recv_sem=sum_recv.at[c],
             device_id={"tp": 1 - t}, device_id_type=MESH,
         )
 
     def keep_copy(c):
-        return pltpu.make_async_copy(part.at[c, own_half], own_out_ref.at[:, wide_cut(c)], keep_sem.at[c])
+        return pltpu.make_async_copy(part.at[c, own_half], out_ref.at[:, wide_cut(c)], keep_sem.at[c])
+
+    def finish(c):
+        sum_copy(c).wait_recv()
+        total = part[c, own_half, :].astype(jnp.float32) + other[c].astype(jnp.float32)
+        part[c, own_half, :] = total.astype(jnp.bfloat16)
+        keep_copy(c).start()
 
     for g in range(cuts):
         share = PIECES // cuts
@@ -275,15 +284,15 @@
             else:
                 part[c] = term.astype(jnp.bfloat16)
                 sum_copy(c).start()
-                keep_copy(c).start()
+
+                @pl.when(c >= BEHIND)
+                def _():
+                    finish(c - BEHIND)
 
         loop(0, wide_count, one_width)
 
-    def finish(c):
-        keep_copy(c).wait()
-        sum_copy(c).wait_recv()
-
-    loop(0, wide_count, finish)
+    loop(wide_count - BEHIND, wide_count, finish)
+    loop(0, wide_count, lambda c: keep_copy(c).wait())
 
     for g in range(shared):
         pair_copy(g).wait_send()
@@ -301,6 +310,18 @@
     for c in range(cuts):
         loop(1, n, lambda e: a2a_copy(c, e).wait_send())
     loop(0, wide_count, lambda c: sum_copy(c).wait_send())
+
+
+def copy_kernel(from_ref, to_ref, sem):
+    rows = from_ref.shape[0] // COPIES
+    copies = [
+        pltpu.make_async_copy(from_ref.at[pl.ds(i * rows, rows)], to_ref.at[pl.ds(i * rows, rows)], sem.at[i])
+        for i in range(COPIES)
+    ]
+    for copy in copies:
+        copy.start()
+    for copy in copies:
+        copy.wait()
 
 
 def fused_shards(segment_ids, relayout, queries, keys, values, out_weight):
@@ -314,11 +335,11 @@
     bf16, f32 = jnp.bfloat16, jnp.float32
     dma = pltpu.SemaphoreType.DMA
     vmem = pl.BlockSpec(memory_space=pltpu.VMEM)
-    own, other = pl.pallas_call(
+    result = pl.pallas_call(
         functools.partial(fused_kernel, n, reach),
-        out_shape=[jax.ShapeDtypeStruct((rows // 2, width), bf16)] * 2,
+        out_shape=jax.ShapeDtypeStruct((rows // 2, width), bf16),
         in_specs=[vmem] * 5 + [pl.BlockSpec(memory_space=pl.ANY)],
-        out_specs=[pl.BlockSpec(memory_space=pl.ANY)] * 2,
+        out_specs=pl.BlockSpec(memory_space=pl.ANY),
         scratch_shapes=[
             pltpu.VMEM((n, rows), jnp.int32),
             pltpu.VMEM((n, rows), jnp.int32),
@@ -336,6 +357,7 @@
             pltpu.VMEM((CUTS, rows, depth), bf16),
             pltpu.VMEM((wide_count, rows, WIDE), f32),
             pltpu.VMEM((wide_count, rows, WIDE), bf16),
+            pltpu.VMEM((wide_count, rows // 2, WIDE), bf16),
             pltpu.VMEM(out_weight.shape, bf16),
             dma((PIECES,)),
             dma((shared,)),
@@ -354,7 +376,13 @@
             collective_id=0, has_side_effects=True, vmem_limit_bytes=63 * 1024 * 1024
         ),
     )(segment_ids.reshape(-1, 128), relayout.reshape(-1, 128), queries, keys, values, out_weight)
-    return (own.astype(f32) + other.astype(f32)).astype(bf16)
+    return pl.pallas_call(
+        copy_kernel,
+        out_shape=jax.ShapeDtypeStruct(result.shape, bf16),
+        in_specs=[pl.BlockSpec(memory_space=pl.ANY)],
+        out_specs=pl.BlockSpec(memory_space=pl.ANY),
+        scratch_shapes=[dma((COPIES,))],
+    )(result)
 
 
 def shards(segment_ids, relayout, queries, keys, values, out_weight):

time: 64.2 us -> 126 us (1.96)
  Pallas kernels: 60 us -> 126 us
  other arithmetic: 4.04 us -> 0 us
    pallas_call x1 -> x2, Pallas kernels: 60 us -> 126 us  [the longest x1 64.7 us: fused_shards(): pl.pallas_call(copy_kernel, out_shape=jax.ShapeDtypeStruct(result.shape,...]
    convert_element_type x1 -> x0, other arithmetic: 4.04 us -> none  [fused_shards(): return (own.astype(f32) + other.astype(f32)).astype(bf16)]
where the time goes in v3:
time: 126 us
  Pallas kernels  126 us (100%)
    pallas_call x1, Pallas kernels, fused_shards(): pl.pallas_call(copy_kernel, out_shape=jax.ShapeDtypeStruct(result.shape,...  64.7 us
    pallas_call x1, Pallas kernels, fused_shards(): pl.pallas_call(functools.partial(fused_kernel, n, reach), out_shape=jax.S...  61.5 us

profile of v3, /device:TPU:15, one launch (start us, length us, event | category | flops | bytes accessed | tf_op | source)
XLA Modules:
  0.0 126.2 jit_solution(2183194384491497096)
XLA Ops:
  0.0 61.5 %shard_map.64.from_ref = bf16[128,8192]{1,0:T(8,128)(2,1)} custom-call(s32[32,128]{1,0:T(8,128)} %bitcast.2, s32[32,128]{1,0:T(8,128)} %bitcast.3, bf16[256,2048]{1,0:T(8,128)(2,1)} %q_ref.1, bf16[128,512]{1,0:T(8,128)(2,1)} %k_ref.1, bf16[128,512]{1,0:T(8,128)(2,1)} %v_ref.1, bf16[2048,8192]{1,0:T(8,128)(2,1)} %w_hbm.1), custom_call_target="tpu_custom_call" | custom-call | tf_op jit(solution)/shard_map/pallas_call | solution.py:338
  61.5 64.7 %shard_map.65 = bf16[128,8192]{1,0:T(8,128)(2,1)} custom-call(bf16[128,8192]{1,0:T(8,128)(2,1)} %shard_map.64.from_ref), custom_call_target="tpu_custom_call" | custom-call | tf_op jit(solution)/shard_map/pallas_call | solution.py:379

commit v4 on v3

--- a/solution.py
+++ b/solution.py
@@ -205,13 +205,13 @@
 
     ones = jnp.ones((rows, HD), jnp.bfloat16)
 
-    def one_head(g, h, to):
-        q = q_sorted[:, pl.ds(pl.multiple_of(h * HD, HD), HD)]
-        q = jnp.concatenate([q, query_tag[...]], axis=1)
+    def some_heads(g, h, to):
+        q = [q_sorted[:, pl.ds(pl.multiple_of((h + k) * HD, HD), HD)] for k in range(TOGETHER)]
+        q = jnp.concatenate([jnp.concatenate([x, query_tag[...]], axis=1) for x in q], axis=0)
         scores = [
             dot_nt(q, jnp.concatenate([kv[d, g, :, 0:HD], key_tag[d]], axis=1)) for d in range(reach + 1)
         ]
-        is_own = own_first[...] > 0.5
+        is_own = jnp.concatenate([own_first[...]] * TOGETHER, axis=0) > 0.5
         scores = [jnp.where(is_own, scores[0], scores[reach])] + scores[1:reach]
         peak = jnp.max(functools.reduce(jnp.maximum, scores), axis=1, keepdims=True)
         expo = [jnp.exp2((x - peak) * factor) for x in scores]
@@ -225,9 +225,11 @@
                 for d, x in enumerate(expo)
             ],
         )
-        sendb[to, :, pl.ds(pl.multiple_of((h - to * cut_heads) * HD, HD), HD)] = (
-            update[:, 0:HD] / update[:, HD : 2 * HD]
-        ).astype(jnp.bfloat16)
+        attn = (update[:, 0:HD] / update[:, HD : 2 * HD]).astype(jnp.bfloat16)
+        for k in range(TOGETHER):
+            sendb[to, :, pl.ds(pl.multiple_of((h + k - to * cut_heads) * HD, HD), HD)] = attn[
+                k * rows : (k + 1) * rows
+            ]
 
     for c in range(cuts):
         g = c * cut_heads // per_shared
@@ -242,8 +244,7 @@
             w_step = PIECES * TOGETHER // (cuts * cut_heads)
             first = (c * cut_heads // TOGETHER + i) * w_step
             loop(first, first + w_step, lambda j: w_copy(j).start())
-            for k in range(TOGETHER):
-                one_head(g, c * cut_heads + i * TOGETHER + k, c)
+            some_heads(g, c * cut_heads + i * TOGETHER, c)
 
         loop(0, cut_heads // TOGETHER, heads)
         loop(1, n, lambda e: a2a_copy(c, e).start())
@@ -269,20 +270,20 @@
         part[c, own_half, :] = total.astype(jnp.bfloat16)
         keep_copy(c).start()
 
-    for g in range(cuts):
+    for first, last in ((0, cuts - 1), (cuts - 1, cuts)):
         share = PIECES // cuts
-        loop(g * share, (g + 1) * share, lambda i: w_copy(i).wait())
-        loop(1, n, lambda e: a2a_copy(g, e).wait_recv())
-        mixed[...] = dot(recv_perm[...], arr[g]).astype(jnp.bfloat16)
+        loop(first * share, last * share, lambda i: w_copy(i).wait())
+        for c in range(first, last):
+            loop(1, n, lambda e: a2a_copy(c, e).wait_recv())
+            mixed[:, c * depth : (c + 1) * depth] = dot(recv_perm[...], arr[c]).astype(jnp.bfloat16)
+        deep = slice(first * depth, last * depth)
 
         def one_width(c):
-            term = dot(mixed[...], wbuf[g * depth : (g + 1) * depth, wide_cut(c)])
-            if g > 0:
-                term = term + acc[c]
-            if g < cuts - 1:
+            term = dot(mixed[:, deep], wbuf[deep, wide_cut(c)])
+            if last < cuts:
                 acc[c] = term
             else:
-                part[c] = term.astype(jnp.bfloat16)
+                part[c] = (acc[c] + term).astype(jnp.bfloat16)
                 sum_copy(c).start()
 
                 @pl.when(c >= BEHIND)
@@ -312,16 +313,25 @@
     loop(0, wide_count, lambda c: sum_copy(c).wait_send())
 
 
-def copy_kernel(from_ref, to_ref, sem):
+def copy_kernel(from_ref, to_ref, held, in_sem, out_sem):
     rows = from_ref.shape[0] // COPIES
-    copies = [
-        pltpu.make_async_copy(from_ref.at[pl.ds(i * rows, rows)], to_ref.at[pl.ds(i * rows, rows)], sem.at[i])
-        for i in range(COPIES)
-    ]
-    for copy in copies:
-        copy.start()
-    for copy in copies:
-        copy.wait()
+
+    def cut(i):
+        return pl.ds(i * rows, rows)
+
+    def take(i):
+        return pltpu.make_async_copy(from_ref.at[cut(i)], held.at[cut(i)], in_sem.at[i])
+
+    def give(i):
+        return pltpu.make_async_copy(held.at[cut(i)], to_ref.at[cut(i)], out_sem.at[i])
+
+    for i in range(COPIES):
+        take(i).start()
+    for i in range(COPIES):
+        take(i).wait()
+        give(i).start()
+    for i in range(COPIES):
+        give(i).wait()
 
 
 def fused_shards(segment_ids, relayout, queries, keys, values, out_weight):
@@ -352,7 +362,7 @@
             pltpu.VMEM((rows, rows), bf16),
             pltpu.VMEM((n, rows), f32),
             pltpu.VMEM(queries.shape, bf16),
-            pltpu.VMEM((rows, depth), bf16),
+            pltpu.VMEM(queries.shape, bf16),
             pltpu.VMEM((CUTS, rows, depth), bf16),
             pltpu.VMEM((CUTS, rows, depth), bf16),
             pltpu.VMEM((wide_count, rows, WIDE), f32),
@@ -381,7 +391,7 @@
         out_shape=jax.ShapeDtypeStruct(result.shape, bf16),
         in_specs=[pl.BlockSpec(memory_space=pl.ANY)],
         out_specs=pl.BlockSpec(memory_space=pl.ANY),
-        scratch_shapes=[dma((COPIES,))],
+        scratch_shapes=[pltpu.VMEM(result.shape, bf16), dma((COPIES,)), dma((COPIES,))],
     )(result)
 
 

time: 126 us -> 66.6 us (0.53)
  Pallas kernels: 126 us -> 66.4 us
    pallas_call x1, Pallas kernels: 64.7 us -> 2.39 us  [fused_shards(): pl.pallas_call(copy_kernel, out_shape=jax.ShapeDtypeStruct(result.shape,...]
    pallas_call x1, Pallas kernels: 61.5 us -> 64 us  [fused_shards(): pl.pallas_call(functools.partial(fused_kernel, n, reach), out_shape=jax.S...]
where the time goes in v4:
time: 66.6 us; the launch traced here: 66.4 us
  Pallas kernels  66.4 us (100%)
    pallas_call x1, Pallas kernels, fused_shards(): pl.pallas_call(functools.partial(fused_kernel, n, reach), out_shape=jax.S...  64 us
    pallas_call x1, Pallas kernels, fused_shards(): pl.pallas_call(copy_kernel, out_shape=jax.ShapeDtypeStruct(result.shape,...  2.39 us

profile of v4, /device:TPU:15, one launch (start us, length us, event | category | flops | bytes accessed | tf_op | source)
XLA Modules:
  0.0 66.4 jit_solution(11215392222668499662)
XLA Ops:
  0.0 64.0 %shard_map.64.from_ref = bf16[128,8192]{1,0:T(8,128)(2,1)} custom-call(s32[32,128]{1,0:T(8,128)} %bitcast.2, s32[32,128]{1,0:T(8,128)} %bitcast.3, bf16[256,2048]{1,0:T(8,128)(2,1)} %q_ref.1, bf16[128,512]{1,0:T(8,128)(2,1)} %k_ref.1, bf16[128,512]{1,0:T(8,128)(2,1)} %v_ref.1, bf16[2048,8192]{1,0:T(8,128)(2,1)} %w_hbm.1), custom_call_target="tpu_custom_call" | custom-call | tf_op jit(solution)/shard_map/pallas_call | solution.py:348
  64.0 2.4 %shard_map.65 = bf16[128,8192]{1,0:T(8,128)(2,1)} custom-call(bf16[128,8192]{1,0:T(8,128)(2,1)} %shard_map.64.from_ref), custom_call_target="tpu_custom_call" | custom-call | tf_op jit(solution)/shard_map/pallas_call | solution.py:389

commit v5 on v3

--- a/solution.py
+++ b/solution.py
@@ -16,8 +16,9 @@
 PIECES = 32
 CUTS = 4
 TOGETHER = 2
-BEHIND = 3
+BEHIND = 8
 COPIES = 8
+SPREAD = 7
 
 
 def dot(a, b):
@@ -193,7 +194,7 @@
         relay(g)
 
     def a2a_copy(g, e):
-        target = lax.rem(s + e, n)
+        target = lax.rem(s + SPREAD * e, n)
         return pltpu.make_async_remote_copy(
             src_ref=sendb.at[g, pl.ds(pl.multiple_of(target * per_pair, per_pair), per_pair)],
             dst_ref=arr.at[g, pl.ds(pl.multiple_of(s * per_pair, per_pair), per_pair)],
@@ -203,7 +204,7 @@
 
     factor = HD ** (-0.5) * 1.4426950408889634
 
-    ones = jnp.ones((rows, HD), jnp.bfloat16)
+    all_ones = jnp.ones(((reach + 1) * rows, HD), jnp.bfloat16)
 
     def one_head(g, h, to):
         q = q_sorted[:, pl.ds(pl.multiple_of(h * HD, HD), HD)]
@@ -218,13 +219,9 @@
         expo = (
             [jnp.where(is_own, expo[0], 0.0)] + expo[1:] + [jnp.where(is_own, 0.0, expo[0])]
         )
-        update = functools.reduce(
-            jnp.add,
-            [
-                dot(x.astype(jnp.bfloat16), jnp.concatenate([kv[d, g, :, HD : 2 * HD], ones], axis=1))
-                for d, x in enumerate(expo)
-            ],
-        )
+        weight = jnp.concatenate([x.astype(jnp.bfloat16) for x in expo], axis=1)
+        value = jnp.concatenate([kv[d, g, :, HD : 2 * HD] for d in range(reach + 1)], axis=0)
+        update = dot(weight, jnp.concatenate([value, all_ones], axis=1))
         sendb[to, :, pl.ds(pl.multiple_of((h - to * cut_heads) * HD, HD), HD)] = (
             update[:, 0:HD] / update[:, HD : 2 * HD]
         ).astype(jnp.bfloat16)
@@ -312,16 +309,25 @@
     loop(0, wide_count, lambda c: sum_copy(c).wait_send())
 
 
-def copy_kernel(from_ref, to_ref, sem):
+def copy_kernel(from_ref, to_ref, held, in_sem, out_sem):
     rows = from_ref.shape[0] // COPIES
-    copies = [
-        pltpu.make_async_copy(from_ref.at[pl.ds(i * rows, rows)], to_ref.at[pl.ds(i * rows, rows)], sem.at[i])
-        for i in range(COPIES)
-    ]
-    for copy in copies:
-        copy.start()
-    for copy in copies:
-        copy.wait()
+
+    def cut(i):
+        return pl.ds(i * rows, rows)
+
+    def take(i):
+        return pltpu.make_async_copy(from_ref.at[cut(i)], held.at[cut(i)], in_sem.at[i])
+
+    def give(i):
+        return pltpu.make_async_copy(held.at[cut(i)], to_ref.at[cut(i)], out_sem.at[i])
+
+    for i in range(COPIES):
+        take(i).start()
+    for i in range(COPIES):
+        take(i).wait()
+        give(i).start()
+    for i in range(COPIES):
+        give(i).wait()
 
 
 def fused_shards(segment_ids, relayout, queries, keys, values, out_weight):
@@ -381,7 +387,7 @@
         out_shape=jax.ShapeDtypeStruct(result.shape, bf16),
         in_specs=[pl.BlockSpec(memory_space=pl.ANY)],
         out_specs=pl.BlockSpec(memory_space=pl.ANY),
-        scratch_shapes=[dma((COPIES,))],
+        scratch_shapes=[pltpu.VMEM(result.shape, bf16), dma((COPIES,)), dma((COPIES,))],
     )(result)
 
 

time: 126 us -> 64.7 us (0.51)
  the two profiles are of different devices: /device:TPU:15 before, /device:TPU:3 now
where the time goes in v5:
time: 64.7 us; the launch traced here: 64.5 us
  Pallas kernels  64.5 us (100%)
    pallas_call x1, Pallas kernels, fused_shards(): pl.pallas_call(functools.partial(fused_kernel, n, reach), out_shape=jax.S...  62.1 us
    pallas_call x1, Pallas kernels, fused_shards(): pl.pallas_call(copy_kernel, out_shape=jax.ShapeDtypeStruct(result.shape,...  2.39 us

profile of v5, /device:TPU:3, one launch (start us, length us, event | category | flops | bytes accessed | tf_op | source)
XLA Modules:
  0.0 64.5 jit_solution(6894555245122645612)
XLA Ops:
  0.0 62.1 %shard_map.64.from_ref = bf16[128,8192]{1,0:T(8,128)(2,1)} custom-call(s32[32,128]{1,0:T(8,128)} %bitcast.2, s32[32,128]{1,0:T(8,128)} %bitcast.3, bf16[256,2048]{1,0:T(8,128)(2,1)} %q_ref.1, bf16[128,512]{1,0:T(8,128)(2,1)} %k_ref.1, bf16[128,512]{1,0:T(8,128)(2,1)} %v_ref.1, bf16[2048,8192]{1,0:T(8,128)(2,1)} %w_hbm.1), custom_call_target="tpu_custom_call" | custom-call | tf_op jit(solution)/shard_map/pallas_call | solution.py:344
  62.1 2.4 %shard_map.65 = bf16[128,8192]{1,0:T(8,128)(2,1)} custom-call(bf16[128,8192]{1,0:T(8,128)(2,1)} %shard_map.64.from_ref), custom_call_target="tpu_custom_call" | custom-call | tf_op jit(solution)/shard_map/pallas_call | solution.py:385

commit v6 on v5

--- a/solution.py
+++ b/solution.py
@@ -18,7 +18,6 @@
 TOGETHER = 2
 BEHIND = 8
 COPIES = 8
-SPREAD = 7
 
 
 def dot(a, b):
@@ -40,9 +39,9 @@
 def fused_kernel(
     n, reach, seg_in, lay_in, q_ref, k_ref, v_ref, w_hbm, out_ref,
     seg_ref, lay_ref, kv, stage, key_tag, query_tag, own_first, send_perm, recv_perm, rank_ref, q_sorted,
-    mixed, sendb, arr, acc, part, other, wbuf,
+    mixed, sendb, passed, arr, acc, part, other, wbuf,
     w_sem, pair_send, pair_recv, far_send, far_recv, near_send, near_recv,
-    a2a_send, a2a_recv, sum_send, sum_recv, keep_sem,
+    deal_send, deal_recv, pass_send, pass_recv, sum_send, sum_recv, keep_sem,
 ):
     s = lax.axis_index("seq")
     t = lax.axis_index("tp")
@@ -193,14 +192,38 @@
     for g in range(1, shared):
         relay(g)
 
-    def a2a_copy(g, e):
-        target = lax.rem(s + SPREAD * e, n)
+    layers = n // reach
+    layer = s // reach
+    layer_rows = reach * per_pair
+    to_place = pl.ds(pl.multiple_of(place * per_pair, per_pair), per_pair)
+
+    def deal_copy(c, e):
+        target = lax.rem(s + e * reach, n)
+        cut = pl.ds(pl.multiple_of(target // reach * layer_rows, layer_rows), layer_rows)
         return pltpu.make_async_remote_copy(
-            src_ref=sendb.at[g, pl.ds(pl.multiple_of(target * per_pair, per_pair), per_pair)],
-            dst_ref=arr.at[g, pl.ds(pl.multiple_of(s * per_pair, per_pair), per_pair)],
-            send_sem=a2a_send.at[g, e], recv_sem=a2a_recv.at[g, e],
+            src_ref=sendb.at[c, cut], dst_ref=passed.at[c, layer],
+            send_sem=deal_send.at[c, e], recv_sem=deal_recv.at[c, e],
             device_id={"seq": target}, device_id_type=MESH,
         )
+
+    def pass_copy(c, e):
+        target = lax.rem(place + e, reach)
+        cut = pl.ds(pl.multiple_of(target * per_pair, per_pair), per_pair)
+        return pltpu.make_async_remote_copy(
+            src_ref=passed.at[c, :, cut], dst_ref=arr.at[c, :, to_place],
+            send_sem=pass_send.at[c, e], recv_sem=pass_recv.at[c, e],
+            device_id={"seq": base + target}, device_id_type=MESH,
+        )
+
+    def deal(c):
+        loop(1, layers, lambda e: deal_copy(c, e).start())
+        keep = pl.ds(pl.multiple_of(layer * layer_rows, layer_rows), layer_rows)
+        passed[c, layer] = sendb[c, keep, :]
+
+    def pass_on(c):
+        loop(1, layers, lambda e: deal_copy(c, e).wait_recv())
+        loop(1, reach, lambda e: pass_copy(c, e).start())
+        arr[c, :, to_place, :] = passed[c, :, to_place, :]
 
     factor = HD ** (-0.5) * 1.4426950408889634
 
@@ -243,9 +266,9 @@
                 one_head(g, c * cut_heads + i * TOGETHER + k, c)
 
         loop(0, cut_heads // TOGETHER, heads)
-        loop(1, n, lambda e: a2a_copy(c, e).start())
-        keep = pl.ds(pl.multiple_of(s * per_pair, per_pair), per_pair)
-        arr[c, keep, :] = sendb[c, keep, :]
+        deal(c)
+        if c >= 2:
+            pass_on(c - 2)
 
     def wide_cut(c):
         return pl.ds(pl.multiple_of(c * WIDE, WIDE), WIDE)
@@ -269,8 +292,10 @@
     for g in range(cuts):
         share = PIECES // cuts
         loop(g * share, (g + 1) * share, lambda i: w_copy(i).wait())
-        loop(1, n, lambda e: a2a_copy(g, e).wait_recv())
-        mixed[...] = dot(recv_perm[...], arr[g]).astype(jnp.bfloat16)
+        if 0 < g < cuts - 1:
+            pass_on(g + 1)
+        loop(1, reach, lambda e: pass_copy(g, e).wait_recv())
+        mixed[...] = dot(recv_perm[...], arr[g].reshape(rows, depth)).astype(jnp.bfloat16)
 
         def one_width(c):
             term = dot(mixed[...], wbuf[g * depth : (g + 1) * depth, wide_cut(c)])
@@ -305,7 +330,8 @@
                 near_copy(g, e, 0).wait_send()
 
     for c in range(cuts):
-        loop(1, n, lambda e: a2a_copy(c, e).wait_send())
+        loop(1, layers, lambda e: deal_copy(c, e).wait_send())
+        loop(1, reach, lambda e: pass_copy(c, e).wait_send())
     loop(0, wide_count, lambda c: sum_copy(c).wait_send())
 
 
@@ -360,7 +386,8 @@
             pltpu.VMEM(queries.shape, bf16),
             pltpu.VMEM((rows, depth), bf16),
             pltpu.VMEM((CUTS, rows, depth), bf16),
-            pltpu.VMEM((CUTS, rows, depth), bf16),
+            pltpu.VMEM((CUTS, n // reach, rows * reach // n, depth), bf16),
+            pltpu.VMEM((CUTS, n // reach, rows * reach // n, depth), bf16),
             pltpu.VMEM((wide_count, rows, WIDE), f32),
             pltpu.VMEM((wide_count, rows, WIDE), bf16),
             pltpu.VMEM((wide_count, rows // 2, WIDE), bf16),
@@ -372,8 +399,10 @@
             dma((shared,)),
             dma((shared, reach)),
             dma((shared, reach)),
-            dma((CUTS, n)),
-            dma((CUTS, n)),
+            dma((CUTS, n // reach)),
+            dma((CUTS, n // reach)),
+            dma((CUTS, reach)),
+            dma((CUTS, reach)),
             dma((wide_count,)),
             dma((wide_count,)),
             dma((wide_count,)),

time: 64.7 us -> 68.1 us (1.053)
  the two profiles are of different devices: /device:TPU:3 before, /device:TPU:9 now
where the time goes in v6:
time: 68.1 us; the launch traced here: 67.9 us
  Pallas kernels  67.9 us (100%)
    pallas_call x1, Pallas kernels, fused_shards(): pl.pallas_call(functools.partial(fused_kernel, n, reach), out_shape=jax.S...  65.5 us
    pallas_call x1, Pallas kernels, fused_shards(): pl.pallas_call(copy_kernel, out_shape=jax.ShapeDtypeStruct(result.shape,...  2.39 us

profile of v6, /device:TPU:9, one launch (start us, length us, event | category | flops | bytes accessed | tf_op | source)
XLA Modules:
  0.0 67.9 jit_solution(4501458302783393667)
XLA Ops:
  0.0 65.5 %shard_map.64.from_ref = bf16[128,8192]{1,0:T(8,128)(2,1)} custom-call(s32[32,128]{1,0:T(8,128)} %bitcast.2, s32[32,128]{1,0:T(8,128)} %bitcast.3, bf16[256,2048]{1,0:T(8,128)(2,1)} %q_ref.1, bf16[128,512]{1,0:T(8,128)(2,1)} %k_ref.1, bf16[128,512]{1,0:T(8,128)(2,1)} %v_ref.1, bf16[2048,8192]{1,0:T(8,128)(2,1)} %w_hbm.1), custom_call_target="tpu_custom_call" | custom-call | tf_op jit(solution)/shard_map/pallas_call | solution.py:370
  65.5 2.4 %shard_map.65 = bf16[128,8192]{1,0:T(8,128)(2,1)} custom-call(bf16[128,8192]{1,0:T(8,128)(2,1)} %shard_map.64.from_ref), custom_call_target="tpu_custom_call" | custom-call | tf_op jit(solution)/shard_map/pallas_call | solution.py:414

commit v7 on v5

--- a/solution.py
+++ b/solution.py
@@ -12,13 +12,12 @@
 HD = 128
 LONGEST_SHARE = 4
 MESH = pl.DeviceIdType.MESH
-WIDE = 512
-PIECES = 32
+WIDE = 1024
+PIECES = 8
 CUTS = 4
 TOGETHER = 2
-BEHIND = 8
+BEHIND = 4
 COPIES = 8
-SPREAD = 7
 
 
 def dot(a, b):
@@ -29,12 +28,12 @@
     return lax.dot_general(a, b, (((1,), (1,)), ((), ())), preferred_element_type=jnp.float32)
 
 
-def loop(low, high, body):
+def loop(low, high, body, unroll=1):
     def step(i, carry):
         body(i)
         return carry
 
-    lax.fori_loop(low, high, step, 0)
+    lax.fori_loop(low, high, step, 0, unroll=unroll)
 
 
 def fused_kernel(
@@ -136,6 +135,7 @@
             kv[e] = jnp.zeros_like(kv[e])
 
     own_out(0)
+    loop(0, PIECES, lambda i: w_copy(i).start())
 
     lines = rows // 128
     for ref, source in ((seg_ref, seg_in), (lay_ref, lay_in)):
@@ -168,7 +168,7 @@
         cut = pl.ds(pl.multiple_of(b * per_pair, per_pair), per_pair)
         send_perm[cut, :] = dot_nt(pick, token).astype(jnp.bfloat16)
 
-    loop(0, n, one_target)
+    loop(0, n, one_target, unroll=4)
 
     def sort_queries(c):
         cut = pl.ds(pl.multiple_of(c * depth, depth), depth)
@@ -181,20 +181,12 @@
     query_tag[...] = jnp.where(document == tag_id.astype(jnp.float32), 0.0, -1e30).astype(jnp.bfloat16)
     own_first[...] = jnp.where(col_id.astype(jnp.float32) <= position, 1.0, 0.0)
 
-    origin = lay_ref[pl.ds(s, 1), :] // rows
-    block_id = lax.broadcasted_iota(jnp.int32, (n, rows), 0)
-    from_block = jnp.where(origin == block_id, 1.0, 0.0)
-    earlier = dot(from_block.astype(jnp.bfloat16), before)
-    rank = jnp.sum(from_block * earlier, axis=0, keepdims=True)
-    slot_of = origin.astype(jnp.float32) * per_pair + rank
-    slot_col = jnp.broadcast_to(slot_of, (rows, rows)).T
-    recv_perm[...] = jnp.where(slot_col == col_id.astype(jnp.float32), 1.0, 0.0).astype(jnp.bfloat16)
 
     for g in range(1, shared):
         relay(g)
 
     def a2a_copy(g, e):
-        target = lax.rem(s + SPREAD * e, n)
+        target = lax.rem(s + e, n)
         return pltpu.make_async_remote_copy(
             src_ref=sendb.at[g, pl.ds(pl.multiple_of(target * per_pair, per_pair), per_pair)],
             dst_ref=arr.at[g, pl.ds(pl.multiple_of(s * per_pair, per_pair), per_pair)],
@@ -236,9 +228,6 @@
                     near_copy(g, e, 0).wait_recv()
 
         def heads(i):
-            w_step = PIECES * TOGETHER // (cuts * cut_heads)
-            first = (c * cut_heads // TOGETHER + i) * w_step
-            loop(first, first + w_step, lambda j: w_copy(j).start())
             for k in range(TOGETHER):
                 one_head(g, c * cut_heads + i * TOGETHER + k, c)
 
@@ -246,6 +235,15 @@
         loop(1, n, lambda e: a2a_copy(c, e).start())
         keep = pl.ds(pl.multiple_of(s * per_pair, per_pair), per_pair)
         arr[c, keep, :] = sendb[c, keep, :]
+
+    origin = lay_ref[pl.ds(s, 1), :] // rows
+    block_id = lax.broadcasted_iota(jnp.int32, (n, rows), 0)
+    from_block = jnp.where(origin == block_id, 1.0, 0.0)
+    earlier = dot(from_block.astype(jnp.bfloat16), before)
+    rank = jnp.sum(from_block * earlier, axis=0, keepdims=True)
+    slot_of = origin.astype(jnp.float32) * per_pair + rank
+    slot_col = jnp.broadcast_to(slot_of, (rows, rows)).T
+    recv_perm[...] = jnp.where(slot_col == col_id.astype(jnp.float32), 1.0, 0.0).astype(jnp.bfloat16)
 
     def wide_cut(c):
         return pl.ds(pl.multiple_of(c * WIDE, WIDE), WIDE)

time: 64.7 us -> 59.3 us (0.917)
  the two profiles are of different devices: /device:TPU:3 before, /device:TPU:15 now
where the time goes in v7:
time: 59.3 us; the launch traced here: 59.1 us
  Pallas kernels  59.1 us (100%)
    pallas_call x1, Pallas kernels, fused_shards(): pl.pallas_call(functools.partial(fused_kernel, n, reach), out_shape=jax.S...  56.7 us
    pallas_call x1, Pallas kernels, fused_shards(): pl.pallas_call(copy_kernel, out_shape=jax.ShapeDtypeStruct(result.shape,...  2.39 us

profile of v7, /device:TPU:15, one launch (start us, length us, event | category | flops | bytes accessed | tf_op | source)
XLA Modules:
  0.0 59.1 jit_solution(16946316333149680456)
XLA Ops:
  0.0 56.7 %shard_map.64.from_ref = bf16[128,8192]{1,0:T(8,128)(2,1)} custom-call(s32[32,128]{1,0:T(8,128)} %bitcast.2, s32[32,128]{1,0:T(8,128)} %bitcast.3, bf16[256,2048]{1,0:T(8,128)(2,1)} %q_ref.1, bf16[128,512]{1,0:T(8,128)(2,1)} %k_ref.1, bf16[128,512]{1,0:T(8,128)(2,1)} %v_ref.1, bf16[2048,8192]{1,0:T(8,128)(2,1)} %w_hbm.1), custom_call_target="tpu_custom_call" | custom-call | tf_op jit(solution)/shard_map/pallas_call | solution.py:342
  56.7 2.4 %shard_map.65 = bf16[128,8192]{1,0:T(8,128)(2,1)} custom-call(bf16[128,8192]{1,0:T(8,128)(2,1)} %shard_map.64.from_ref), custom_call_target="tpu_custom_call" | custom-call | tf_op jit(solution)/shard_map/pallas_call | solution.py:383
